TPU v7x, 512 devices: a whole 4x8x8 slice. The times are simulated.
512 devices in a mesh: res: 64 (over z_hi, x, y), seq: 8 (over z_lo, core).
Axes of the slice: x: 4, y: 8, z: 8 (z_hi: 2, z_lo: 4; z = z_hi * 4 + z_lo), core: 2. Of those that a mesh axis runs over, the one named last changes fastest.
Arguments:
- alignment_features: float32 [512, 512, 256], P('seq', 'res'), may hold values from -8 to 8
- layer_norm_gain: float32 [256], replicated, may hold values from 0.5 to 2
- left_projection_weight: float32 [256, 32], replicated, may hold values from -0.375 to 0.375
- right_projection_weight: float32 [256, 32], replicated, may hold values from -0.375 to 0.375
- output_projection_weight: float32 [1024, 128], replicated, may hold values from -0.1875 to 0.1875
- output_bias_vector: float32 [128], replicated, may hold values from -3 to 3
Outputs:
- pair_tiles: float32 [4, 512, 8, 128], P(None, 'res', 'seq')
All inputs are finite; a program needn't handle non-finite values.
Results may differ from a plain program's by a relative error of at most 0.0003.
Values sent between devices are 32-bit elements; how exact they have to be, the bound alone decides.
A program may use at most 64 MiB of HBM per device.

v0:
```python
import jax
import jax.numpy as jnp
from jax import lax
from jax.sharding import PartitionSpec as P

ROUNDS = 4


def partner_2(value, axis, bit):
    mask = 2**bit
    pairs = [(source, source ^ mask) for source in range(lax.axis_size(axis))]
    return lax.ppermute(value, axis, pairs)


def apply_layer_norm(features, layer_norm_gain):
    row_mean = jnp.mean(features, axis=-1, keepdims=True)
    centered = features - row_mean
    variance = jnp.mean(centered * centered, axis=-1, keepdims=True)
    return centered * lax.rsqrt(variance + 1e-05) * layer_norm_gain


def tile_of(left_part, right_part, output_projection_weight, total_seqs):
    hidden = left_part.shape[2]
    outer_sum = (
        jnp.einsum("sxc,syd->xycd", left_part, right_part, precision=lax.Precision.HIGHEST)
        / total_seqs
    )
    tile_rows = left_part.shape[1]
    tile_cols = right_part.shape[1]
    projected = jnp.dot(
        outer_sum.reshape(tile_rows * tile_cols, hidden * hidden),
        output_projection_weight,
        precision=lax.Precision.HIGHEST,
    )
    return projected.reshape(tile_rows, tile_cols, output_projection_weight.shape[1])


def on_device(
    alignment_features,
    layer_norm_gain,
    left_projection_weight,
    right_projection_weight,
    output_projection_weight,
    output_bias_vector,
):
    local_sequence_rows, residue_block_rows, channel_count = alignment_features.shape
    hidden = left_projection_weight.shape[1]
    total_seqs = local_sequence_rows * lax.axis_size("seq")
    normalized_features = apply_layer_norm(alignment_features, layer_norm_gain)
    flat_rows = normalized_features.reshape(local_sequence_rows * residue_block_rows, channel_count)
    left_proj = jnp.dot(flat_rows, left_projection_weight, precision=lax.Precision.HIGHEST).reshape(
        local_sequence_rows, residue_block_rows, hidden
    )
    right_proj = jnp.dot(
        flat_rows, right_projection_weight, precision=lax.Precision.HIGHEST
    ).reshape(local_sequence_rows, residue_block_rows, hidden)
    round_list = list(range(ROUNDS))
    results = {}
    for step in round_list:
        partner = partner_2(right_proj, "res", step)
        partial_tile = tile_of(left_proj, partner, output_projection_weight, total_seqs)
        results[step] = (
            lax.psum_scatter(partial_tile, "seq", scatter_dimension=1, tiled=True)
            + output_bias_vector
        )
    stacked = jnp.stack([results[step] for step in range(ROUNDS)])
    return stacked


def solution(mesh):
    in_specs = (P("seq", "res", None), P(), P(), P(), P(), P())
    out_specs = P(None, "res", "seq", None)
    return jax.shard_map(
        on_device, mesh=mesh, in_specs=in_specs, out_specs=out_specs, check_vma=False
    )
```

profile of v0, /device:TPU:1, one launch (start us, length us, event | category | flops | bytes accessed | tf_op | source)
XLA Modules:
  0.0 143.4 jit_solution(17794584237299172938)
XLA Ops:
  6.5 0.0 copy-start
  6.5 0.0 all-reduce.7.cloned.1.call-start
  6.5 1.3 reduce_sum.18
  7.8 0.0 copy-done.1
  7.8 0.2 multiply_reduce_fusion
  8.1 0.0 copy-start.4
  8.1 0.0 copy-start.6
  8.1 0.7 copy-done.4
  8.8 0.0 copy-done.6
  8.8 1.3 fusion.13
  10.2 4.0 %collective-permute-start = (f32[64,8,32]{2,1,0:T(8,128)}, f32[64,8,32]{2,1,0:T(8,128)S(1)}, u32[]{:S(2)}, u32[]{:S(2)}) collective-permute-start(f32[64,8,32]{2,1,0:T(8,128)} %fusion.13), channel_id=1, source_target_pairs={{0,8},{8,0},{16,24},{24,16},{32,40},{40,32},{48,56},{56,48},{64,72... | collective-permute-start | bytes 196616 | tf_op jit(solution)/shard_map/ppermute | solution.py:12
  14.2 4.2 %collective-permute-start.1 = (f32[64,8,32]{2,1,0:T(8,128)}, f32[64,8,32]{2,1,0:T(8,128)}, u32[]{:S(2)}, u32[]{:S(2)}) collective-permute-start(f32[64,8,32]{2,1,0:T(8,128)} %fusion.13), channel_id=1, source_target_pairs={{0,16},{8,24},{16,0},{24,8},{32,48},{40,56},{48,32},{56,40},{64,80... | collective-permute-start | bytes 196616 | tf_op jit(solution)/shard_map/ppermute | solution.py:12
  18.4 4.8 %collective-permute-start.2 = (f32[64,8,32]{2,1,0:T(8,128)}, f32[64,8,32]{2,1,0:T(8,128)S(1)}, u32[]{:S(2)}, u32[]{:S(2)}) collective-permute-start(f32[64,8,32]{2,1,0:T(8,128)} %fusion.13), channel_id=1, source_target_pairs={{0,32},{8,40},{16,48},{24,56},{32,0},{40,8},{48,16},{56,24},{64,96... | collective-permute-start | bytes 196616 | tf_op jit(solution)/shard_map/ppermute | solution.py:12
  23.2 3.1 %collective-permute-start.3 = (f32[64,8,32]{2,1,0:T(8,128)}, f32[64,8,32]{2,1,0:T(8,128)S(1)}, u32[]{:S(2)}, u32[]{:S(2)}) collective-permute-start(f32[64,8,32]{2,1,0:T(8,128)} %fusion.13), channel_id=1, source_target_pairs={{0,64},{8,72},{16,80},{24,88},{32,96},{40,104},{48,112},{56,120},{... | collective-permute-start | bytes 196616 | tf_op jit(solution)/shard_map/ppermute | solution.py:12
  26.3 0.6 fusion.12
  26.9 0.1 copy.38
  27.1 0.0 collective-permute-done
  27.1 1.8 %fusion.3 = f32[8,8,32,32]{2,3,0,1:T(8,128)S(1)} fusion(f32[64,8,32,1]{2,1,0,3:T(8,128)S(1)} %bitcast.63, f32[64,8,32]{0,2,1:T(8,128)S(1)} %copy.38), kind=kOutput, calls=%fused_computation.7 | convolution fusion | flops 50397184 | bytes 393216 | tf_op jit(solution)/shard_map/sxc,syd->xycd/dot_general | solution.py:25
  28.9 0.3 copy.39
  29.2 0.5 dot_general.41
  29.7 0.0 collective-permute-done.1
  29.7 2.7 %fusion.2 = f32[8,8,32,32]{2,3,0,1:T(8,128)S(1)} fusion(f32[64,8,32,1]{2,1,0,3:T(8,128)} %bitcast.7, f32[64,8,32]{0,2,1:T(8,128)S(1)} %copy.38), kind=kOutput, calls=%fused_computation.5 | convolution fusion | flops 50397184 | bytes 393216 | tf_op jit(solution)/shard_map/sxc,syd->xycd/dot_general | solution.py:25
  32.5 0.3 copy.43
  32.8 0.5 dot_general.44
  33.3 0.0 copy-done
  33.3 1.1 fusion.10
  34.4 0.4 fusion.8
  34.8 6.8 %collective-permute-done.2 = f32[64,8,32]{2,1,0:T(8,128)S(1)} collective-permute-done((f32[64,8,32]{2,1,0:T(8,128)}, f32[64,8,32]{2,1,0:T(8,128)S(1)}, u32[]{:S(2)}, u32[]{:S(2)}) %collective-permute-start.2) | collective-permute-done | bytes 65568 | tf_op jit(solution)/shard_map/ppermute | solution.py:12
  41.6 1.8 %fusion.1 = f32[8,8,32,32]{2,3,0,1:T(8,128)S(1)} fusion(f32[64,8,32,1]{2,1,0,3:T(8,128)S(1)} %bitcast.62, f32[64,8,32]{0,2,1:T(8,128)S(1)} %copy.38), kind=kOutput, calls=%fused_computation.3 | convolution fusion | flops 50397184 | bytes 393216 | tf_op jit(solution)/shard_map/sxc,syd->xycd/dot_general | solution.py:25
  43.4 0.3 copy.47
  43.8 0.5 dot_general.47
  44.3 0.4 fusion.6
  44.7 0.3 copy-done.2
  45.0 0.6 copy.40
  45.6 0.6 copy.44
  46.3 0.6 copy.48
  46.9 0.0 collective-permute-done.3
  46.9 1.8 %fusion = f32[8,8,32,32]{2,3,0,1:T(8,128)S(1)} fusion(f32[64,8,32,1]{2,1,0,3:T(8,128)S(1)} %bitcast.61, f32[64,8,32]{0,2,1:T(8,128)S(1)} %copy.38), kind=kOutput, calls=%fused_computation.1 | convolution fusion | flops 50397184 | bytes 393216 | tf_op jit(solution)/shard_map/sxc,syd->xycd/dot_general | solution.py:25
  48.7 0.3 copy.51
  49.0 0.5 dot_general.50
  49.5 0.4 fusion.4
  50.0 0.6 copy.52
  50.6 0.0 all-reduce.7.cloned.1.call-update
  50.6 1.3 dynamic-slice
  51.9 82.1 %all-reduce.7.cloned.1.call-done = (f32[8,8,128]{2,0,1:T(8,128)}, f32[8,8,128]{2,0,1:T(8,128)}, f32[8,8,128]{2,0,1:T(8,128)}, f32[8,8,128]{2,0,1:T(8,128)}) async-done(((f32[8,8,128]{2,0,1:T(8,128)}, f32[8,8,128]{2,0,1:T(8,128)}, f32[8,8,128]{2,0,1:T(8,128)}, f32[8,8,128]{2,0,1:T(8,128)}), (f32[8,8,128]{2,0,1:T(8,128)}, f32[8,8,128]{2,0,1:T(8,128)}, f32[8,8,128]{2,0,1:T(8,128)}, ...) | async-done | bytes 131088
  133.9 0.7 copy-done.3
  134.6 1.4 fusion.33
  136.0 0.6 pad_maximum_fusion
  (7 shorter events, 0.0 us)
Async XLA Ops:
  6.5 26.8 %copy-start = (f32[1024,128]{1,0:T(8,128)S(1)}, f32[1024,128]{1,0:T(8,128)}, u32[]{:S(2)}) copy-start(f32[1024,128]{1,0:T(8,128)} %param.10) | copy-start | bytes 1572868
  6.5 1.3 copy-start.1
  6.5 127.4 %all-reduce.7.cloned.1.call-start = ((), (), s32[]{:S(2)}) async-start(), calls=%async_computation | async-start | bytes 262144
  8.1 0.8 copy-start.4
  8.1 0.8 copy-start.6
  8.8 17.5 %copy-start.5 = (f32[256,32]{0,1:T(8,128)S(1)}, f32[256,32]{0,1:T(8,128)}, u32[]{:S(2)}) copy-start(f32[256,32]{0,1:T(8,128)} %param.8) | copy-start | bytes 98308
  10.2 16.9 %collective-permute-start = (f32[64,8,32]{2,1,0:T(8,128)}, f32[64,8,32]{2,1,0:T(8,128)S(1)}, u32[]{:S(2)}, u32[]{:S(2)}) collective-permute-start(f32[64,8,32]{2,1,0:T(8,128)} %fusion.13), channel_id=1, source_target_pairs={{0,8},{8,0},{16,24},{24,16},{32,40},{40,32},{48,56},{56,48},{64,72... | collective-permute-start | bytes 196616 | tf_op jit(solution)/shard_map/ppermute | solution.py:12
  14.2 15.5 %collective-permute-start.1 = (f32[64,8,32]{2,1,0:T(8,128)}, f32[64,8,32]{2,1,0:T(8,128)}, u32[]{:S(2)}, u32[]{:S(2)}) collective-permute-start(f32[64,8,32]{2,1,0:T(8,128)} %fusion.13), channel_id=1, source_target_pairs={{0,16},{8,24},{16,0},{24,8},{32,48},{40,56},{48,32},{56,40},{64,80... | collective-permute-start | bytes 196616 | tf_op jit(solution)/shard_map/ppermute | solution.py:12
  18.4 23.2 %collective-permute-start.2 = (f32[64,8,32]{2,1,0:T(8,128)}, f32[64,8,32]{2,1,0:T(8,128)S(1)}, u32[]{:S(2)}, u32[]{:S(2)}) collective-permute-start(f32[64,8,32]{2,1,0:T(8,128)} %fusion.13), channel_id=1, source_target_pairs={{0,32},{8,40},{16,48},{24,56},{32,0},{40,8},{48,16},{56,24},{64,96... | collective-permute-start | bytes 196616 | tf_op jit(solution)/shard_map/ppermute | solution.py:12
  23.2 23.7 %collective-permute-start.3 = (f32[64,8,32]{2,1,0:T(8,128)}, f32[64,8,32]{2,1,0:T(8,128)S(1)}, u32[]{:S(2)}, u32[]{:S(2)}) collective-permute-start(f32[64,8,32]{2,1,0:T(8,128)} %fusion.13), channel_id=1, source_target_pairs={{0,64},{8,72},{16,80},{24,88},{32,96},{40,104},{48,112},{56,120},{... | collective-permute-start | bytes 196616 | tf_op jit(solution)/shard_map/ppermute | solution.py:12
  44.3 0.8 copy-start.2
  133.9 0.7 copy-start.3
Sparse Core Ops, SparseCore 0:
  50.7 83.1 all-reduce.6
where the time goes:
time: 145 us; the launch traced here: 143 us
  waiting for transfers between devices  88.9 us (61%)
  starting transfers between devices  16.1 us (11%)
  between operations  13.6 us (9%)
  matrix products  12.5 us (9%)
  local copies, waits for them, and re-layouts  8.86 us (6%)
  other arithmetic  3.47 us (2%)
    unnamed x2, waiting for transfers between devices  82.1 us
    ppermute x4, starting transfers between devices, partner_2(): return lax.ppermute(value, axis, pairs)  16.1 us
    dot_general x4, matrix products, tile_of(): jnp.einsum('sxc,syd->xycd', left_part, right_part, precision=lax.Precisio...  8.14 us
    ppermute x4, waiting for transfers between devices, partner_2(): return lax.ppermute(value, axis, pairs)  6.81 us
    dot_general x8, local copies, waits for them, and re-layouts, tile_of(): jnp.dot(outer_sum.reshape(tile_rows * tile_cols, hidden * hidden), output...  4.44 us
    unnamed x15, local copies, waits for them, and re-layouts  2.98 us
  transfers between devices with their start and end apart: 5, of which 2 were waited for; matrix products, arithmetic and copies ran while one was open for 10% of the time, Pallas kernels for 0%

commit v1 on v0

v1 whole, which is shorter than its diff:
```python
import jax
import jax.numpy as jnp
from jax import lax
from jax.experimental import pallas as pl
from jax.experimental.pallas import tpu as pltpu
from jax.sharding import PartitionSpec as P

ROUNDS = 4
CHUNKS = 4
ROUND_ORDER = (3, 0, 1, 2)


def split(value):
    high = value.astype(jnp.bfloat16)
    low = (value - high.astype(jnp.float32)).astype(jnp.bfloat16)
    return high, low


def matmul(a, b):
    return lax.dot_general(a, b, (((1,), (0,)), ((), ())), preferred_element_type=jnp.float32)


def matmul_nt(a, b):
    return lax.dot_general(a, b, (((1,), (1,)), ((), ())), preferred_element_type=jnp.float32)


def group_index(rows, width):
    return lax.broadcasted_iota(jnp.int32, (rows, 128), 1) // width


def pick(parts, group):
    result = parts[-1]
    for index in range(len(parts) - 2, -1, -1):
        result = jnp.where(group == index, parts[index], result)
    return result


def kernel(
    features_hbm,
    gain_hbm,
    left_hbm,
    right_hbm,
    weight_hbm,
    bias_hbm,
    out_ref,
    features,
    gain,
    left_weight,
    right_weight,
    weight,
    bias,
    in_sem,
    proj_high,
    proj_low,
    weight_split,
    left_rows,
    right_rows,
    left_turned,
    left_parts,
    right_mine,
    right_got,
    outer,
    tiles,
    sums,
    right_send_sem,
    right_recv_sem,
    sum_send_sem,
    sum_recv_sem,
):
    rows = features.shape[0]
    chunk_rows = rows // CHUNKS
    chunk_seqs = chunk_rows // 8
    local_seqs = rows // 8
    hidden = 32
    seq_devices = 8
    total_seqs = local_seqs * seq_devices

    block = lax.axis_index("res")
    seq = lax.axis_index("seq")

    def partner(step):
        mask = 1 << step
        return block + mask - 2 * mask * ((block // mask) % 2)

    def peer(offset):
        return (seq + offset) % seq_devices

    loads = []
    for index, (source, target) in enumerate(
        ((left_hbm, left_weight), (right_hbm, right_weight), (gain_hbm, gain))
    ):
        loads.append(pltpu.make_async_copy(source, target, in_sem.at[index]))
    chunk_loads = []
    for chunk in range(CHUNKS):
        part = pl.ds(chunk * chunk_rows, chunk_rows)
        chunk_loads.append(
            pltpu.make_async_copy(features_hbm.at[part], features.at[part], in_sem.at[5 + chunk])
        )
    weight_load = pltpu.make_async_copy(weight_hbm, weight, in_sem.at[3])
    bias_load = pltpu.make_async_copy(bias_hbm, bias, in_sem.at[4])
    for copy in loads + chunk_loads + [weight_load, bias_load]:
        copy.start()

    barrier = pltpu.get_barrier_semaphore()
    for step in range(ROUNDS):
        pl.semaphore_signal(barrier, inc=1, device_id=(partner(step), seq))
    for offset in range(1, seq_devices):
        pl.semaphore_signal(barrier, inc=1, device_id=(block, peer(offset)))

    for copy in loads:
        copy.wait()
    left_high, left_low = split(left_weight[...] * gain[...])
    right_high, right_low = split(right_weight[...] * gain[...])
    proj_high[...] = jnp.concatenate([left_high] * 4 + [right_high] * 4, axis=0)
    proj_low[...] = jnp.concatenate([left_low] * 4 + [right_low] * 4, axis=0)

    def right_copy(step, chunk):
        part = pl.ds(chunk * chunk_seqs, chunk_seqs)
        return pltpu.make_async_remote_copy(
            src_ref=right_mine.at[part],
            dst_ref=right_got.at[step, part],
            send_sem=right_send_sem.at[step, chunk],
            recv_sem=right_recv_sem.at[step, chunk],
            device_id=(partner(step), seq),
        )

    chunk_group = group_index(chunk_seqs, hidden)
    for chunk in range(CHUNKS):
        chunk_loads[chunk].wait()
        part = pl.ds(chunk * chunk_rows, chunk_rows)
        values = features[part]
        centered = values - jnp.mean(values, axis=1, keepdims=True)
        variance = jnp.mean(centered * centered, axis=1, keepdims=True)
        high, low = split(centered * lax.rsqrt(variance + 1e-05))
        projected = (
            matmul_nt(high, proj_low[...]) + matmul_nt(low, proj_high[...])
        ) + matmul_nt(high, proj_high[...])
        left_rows[part] = projected[:, :128]
        right_rows[part] = projected[:, 128:]
        for half in range(2):
            lanes = [
                right_rows[pl.ds(chunk * chunk_rows + half * 4 + x, chunk_seqs, stride=8), :]
                for x in range(4)
            ]
            right_mine[pl.ds(chunk * chunk_seqs, chunk_seqs), pl.ds(half * 128, 128)] = pick(
                lanes, chunk_group
            )
        if chunk == 0:
            pl.semaphore_wait(barrier, ROUNDS + seq_devices - 1)
        for step in (2, 1, 0, 3):
            right_copy(step, chunk).start()

    seq_group = group_index(local_seqs, hidden)
    for half in range(2):
        lanes = [left_rows[pl.ds(half * 4 + x, local_seqs, stride=8), :] for x in range(4)]
        left_half = pick(lanes, seq_group) * (1.0 / total_seqs)
        left_turned[pl.ds(half * 128, 128), :] = jnp.concatenate([left_half, left_half], axis=0).T
    left_columns = jnp.concatenate(
        [left_turned[pl.ds(c, 8, stride=hidden), :] for c in range(hidden)], axis=0
    )
    turned_high, turned_low = split(left_columns)
    left_parts[...] = jnp.concatenate([turned_high, turned_low], axis=1)

    weight_load.wait()
    bias_load.wait()
    weight_high, weight_low = split(weight[...])
    weight_split[...] = jnp.concatenate([weight_high, weight_low], axis=1)

    def sum_copy(step, offset):
        return pltpu.make_async_remote_copy(
            src_ref=tiles.at[step, peer(offset)],
            dst_ref=sums.at[step, offset - 1],
            send_sem=sum_send_sem.at[step, offset - 1],
            recv_sem=sum_recv_sem.at[step, offset - 1],
            device_id=(block, peer(offset)),
        )

    group = group_index(8, hidden)
    for step in ROUND_ORDER:
        for chunk in range(CHUNKS):
            right_copy(step, chunk).wait_recv()
        right_high, right_low = split(right_got[step])
        outer[...] = matmul(
            left_parts[...],
            jnp.concatenate([right_high, right_low, right_high, right_low], axis=0),
        )
        pieces = []
        for y_half in range(2):
            columns = [[None] * 8 for _ in range(4)]
            for c_quad in range(8):
                turned = [
                    outer[pl.ds((c_quad * 4 + i) * 8, 8), pl.ds(y_half * 128, 128)]
                    for i in range(4)
                ]
                turned = [turned[0]] + [pltpu.roll(turned[i], 32 * i, 1) for i in range(1, 4)]
                for y in range(4):
                    mixed = pick([turned[(g - y) % 4] for g in range(4)], group)
                    if y:
                        mixed = pltpu.roll(mixed, 128 - 32 * y, 1)
                    columns[y][c_quad] = mixed
            for y in range(4):
                pieces.append(jnp.concatenate(columns[y], axis=1))
        flat_high, flat_low = split(jnp.concatenate(pieces, axis=0))
        product = matmul(jnp.concatenate([flat_high, flat_low], axis=0), weight_split[...])
        total = (product[64:, 128:] + product[64:, :128]) + (product[:64, 128:] + product[:64, :128])
        tiles[step] = total.reshape(8, 8, 128)
        for offset in range(1, seq_devices):
            sum_copy(step, offset).start()

    for step in ROUND_ORDER:
        for offset in range(1, seq_devices):
            sum_copy(step, offset).wait_recv()
        total = tiles[step, seq] + bias[...]
        for offset in range(1, seq_devices):
            total = total + sums[step, offset - 1]
        out_ref[step] = total

    for step in range(ROUNDS):
        for chunk in range(CHUNKS):
            right_copy(step, chunk).wait_send()
        for offset in range(1, seq_devices):
            sum_copy(step, offset).wait_send()


def on_device(features, gain, left_weight, right_weight, weight, bias):
    local_seqs, residues, channels = features.shape
    rows = local_seqs * residues
    f32, bf16 = jnp.float32, jnp.bfloat16
    dma = pltpu.SemaphoreType.DMA
    out = pl.pallas_call(
        kernel,
        out_shape=jax.ShapeDtypeStruct((ROUNDS, 8, 128), f32),
        in_specs=[pl.BlockSpec(memory_space=pltpu.HBM)] * 6,
        out_specs=pl.BlockSpec(memory_space=pltpu.VMEM),
        scratch_shapes=[
            pltpu.VMEM((rows, channels), f32),
            pltpu.VMEM((1, channels), f32),
            pltpu.VMEM((32, channels), f32),
            pltpu.VMEM((32, channels), f32),
            pltpu.VMEM((1024, 128), f32),
            pltpu.VMEM((1, 128), f32),
            dma((5 + CHUNKS,)),
            pltpu.VMEM((256, channels), bf16),
            pltpu.VMEM((256, channels), bf16),
            pltpu.VMEM((1024, 256), bf16),
            pltpu.VMEM((rows, 128), f32),
            pltpu.VMEM((rows, 128), f32),
            pltpu.VMEM((256, 128), f32),
            pltpu.VMEM((256, 256), bf16),
            pltpu.VMEM((local_seqs, 256), f32),
            pltpu.VMEM((ROUNDS, local_seqs, 256), f32),
            pltpu.VMEM((256, 256), f32),
            pltpu.VMEM((ROUNDS, 8, 8, 128), f32),
            pltpu.VMEM((ROUNDS, 7, 8, 128), f32),
            dma((ROUNDS, CHUNKS)),
            dma((ROUNDS, CHUNKS)),
            dma((ROUNDS, 7)),
            dma((ROUNDS, 7)),
        ],
        compiler_params=pltpu.CompilerParams(
            collective_id=0, has_side_effects=True, vmem_limit_bytes=32 * 1024 * 1024
        ),
    )(
        features.reshape(rows, channels),
        gain.reshape(1, channels),
        left_weight.T,
        right_weight.T,
        weight,
        bias.reshape(1, 128),
    )
    return out.reshape(ROUNDS, 8, 1, 128)


def solution(mesh):
    in_specs = (P("seq", "res", None), P(), P(), P(), P(), P())
    out_specs = P(None, "res", "seq", None)
    return jax.shard_map(
        on_device, mesh=mesh, in_specs=in_specs, out_specs=out_specs, check_vma=False
    )
```

time: 145 us -> 30.9 us (0.21)
  waiting for transfers between devices: 88.9 us -> 0 us
  Pallas kernels: 0 us -> 25.6 us
  starting transfers between devices: 16.1 us -> 0 us
  between operations: 13.6 us -> 0.02 us
  matrix products: 12.5 us -> 0 us
  local copies, waits for them, and re-layouts: 8.86 us -> 4.89 us
  other arithmetic: 3.47 us -> 0 us
    unnamed x2 -> x0, waiting for transfers between devices: 82.1 us -> none
    pallas_call x0 -> x1, Pallas kernels: none -> 25.6 us  [on_device(): pl.pallas_call(kernel, out_shape=jax.ShapeDtypeStruct((ROUNDS, 8, 128), f...]
    ppermute x4 -> x0, starting transfers between devices: 16.1 us -> none  [partner_2(): return lax.ppermute(value, axis, pairs)]
    dot_general x10 -> x0, matrix products: 12.5 us -> none  [the longest x4 8.14 us: tile_of(): jnp.einsum('sxc,syd->xycd', left_part, right_part, precision=lax.Precisio...]
    ppermute x4 -> x0, waiting for transfers between devices: 6.81 us -> none  [partner_2(): return lax.ppermute(value, axis, pairs)]
    dot_general x9 -> x0, local copies, waits for them, and re-layouts: 4.56 us -> none  [the longest x8 4.44 us: tile_of(): jnp.dot(outer_sum.reshape(tile_rows * tile_cols, hidden * hidden), output...]
    another operation x2 -> x0, other arithmetic: 1.96 us -> none  [on_device(): stacked = jnp.stack([results[step] for step in range(ROUNDS)])]
    unnamed x15 -> x13, local copies, waits for them, and re-layouts: 2.98 us -> 4.89 us
  transfers between devices with their start and end apart: 5 -> 0, of which waited for: 2 -> 0; matrix products, arithmetic and copies ran while one was open for 10% -> 0% of each run, Pallas kernels for 0% -> 0%
where the time goes in v1:
time: 30.9 us; the launch traced here: 30.5 us
  Pallas kernels  25.6 us (83%)
  local copies, waits for them, and re-layouts  4.89 us (16%)
    pallas_call x1, Pallas kernels, on_device(): pl.pallas_call(kernel, out_shape=jax.ShapeDtypeStruct((ROUNDS, 8, 128), f...  25.6 us
    unnamed x13, local copies, waits for them, and re-layouts  4.89 us

profile of v1, /device:TPU:1, one launch (start us, length us, event | category | flops | bytes accessed | tf_op | source)
XLA Modules:
  0.0 30.5 jit_solution(13774908047490416716)
XLA Ops:
  0.0 0.0 copy-start.4
  0.0 0.0 copy-start.5
  0.0 0.7 %copy-done.4 = f32[256]{0:T(256)S(1)} copy-done((f32[256]{0:T(256)S(1)}, f32[256]{0:T(256)}, u32[]{:S(2)}) %copy-start.4) | copy-done | bytes 1048
  0.7 0.0 copy-done.5
  0.7 0.0 copy-start
  0.7 1.0 %copy-done = f32[64,8,256]{2,1,0:T(8,128)S(1)} copy-done((f32[64,8,256]{2,1,0:T(8,128)S(1)}, f32[64,8,256]{2,1,0:T(8,128)}, u32[]{:S(2)}) %copy-start) | copy-done | bytes 524312
  1.7 0.0 copy-start.1
  1.7 1.0 %copy-done.1 = f32[1024,128]{1,0:T(8,128)S(1)} copy-done((f32[1024,128]{1,0:T(8,128)S(1)}, f32[1024,128]{1,0:T(8,128)}, u32[]{:S(2)}) %copy-start.1) | copy-done | bytes 524312
  2.8 0.0 copy-start.2
  2.8 0.8 %copy-done.2 = f32[256,32]{0,1:T(8,128)S(1)} copy-done((f32[256,32]{0,1:T(8,128)S(1)}, f32[256,32]{0,1:T(8,128)}, u32[]{:S(2)}) %copy-start.2) | copy-done | bytes 32792
  3.5 0.0 copy-start.3
  3.5 0.8 %copy-done.3 = f32[256,32]{0,1:T(8,128)S(1)} copy-done((f32[256,32]{0,1:T(8,128)S(1)}, f32[256,32]{0,1:T(8,128)}, u32[]{:S(2)}) %copy-start.3) | copy-done | bytes 32792
  4.3 25.6 %shard_map.64 = f32[4,8,128]{2,1,0:T(8,128)S(1)} custom-call(f32[512,256]{1,0:T(8,128)S(1)} %bitcast.8, f32[1,256]{1,0:T(1,128)S(1)} %bitcast.12, f32[32,256]{1,0:T(8,128)S(1)} %bitcast.10, f32[32,256]{1,0:T(8,128)S(1)} %bitcast.11, f32[1024,128]{1,0:T(8,128)S(1)} %copy-done.1, f32[1,128]{1,0:T(1,128)S(1)} %bitcast.13), custom_call_target="tpu_custom_call" | custom-call | tf_op jit(solution)/shard_map/pallas_call | solution.py:230
  29.9 0.6 %copy.9 = f32[4,8,1,128]{3,2,1,0:T(1,128)} copy(f32[4,8,1,128]{3,2,1,0:T(1,128)S(1)} %bitcast.9) | data formatting | bytes 32768
Async XLA Ops:
  0.0 0.7 %copy-start.4 = (f32[256]{0:T(256)S(1)}, f32[256]{0:T(256)}, u32[]{:S(2)}) copy-start(f32[256]{0:T(256)} %param.7) | copy-start | bytes 3076
  0.0 0.7 %copy-start.5 = (f32[128]{0:T(128)S(1)}, f32[128]{0:T(128)}, u32[]{:S(2)}) copy-start(f32[128]{0:T(128)} %param.11) | copy-start | bytes 1540
  0.7 1.0 %copy-start = (f32[64,8,256]{2,1,0:T(8,128)S(1)}, f32[64,8,256]{2,1,0:T(8,128)}, u32[]{:S(2)}) copy-start(f32[64,8,256]{2,1,0:T(8,128)} %param.6) | copy-start | bytes 1572868
  1.7 1.0 %copy-start.1 = (f32[1024,128]{1,0:T(8,128)S(1)}, f32[1024,128]{1,0:T(8,128)}, u32[]{:S(2)}) copy-start(f32[1024,128]{1,0:T(8,128)} %weight_hbm.1) | copy-start | bytes 1572868
  2.8 0.8 %copy-start.2 = (f32[256,32]{0,1:T(8,128)S(1)}, f32[256,32]{0,1:T(8,128)}, u32[]{:S(2)}) copy-start(f32[256,32]{0,1:T(8,128)} %param.8) | copy-start | bytes 98308
  3.5 0.8 %copy-start.3 = (f32[256,32]{0,1:T(8,128)S(1)}, f32[256,32]{0,1:T(8,128)}, u32[]{:S(2)}) copy-start(f32[256,32]{0,1:T(8,128)} %param.9) | copy-start | bytes 98308

commit v2 on v1

--- a/solution.py
+++ b/solution.py
@@ -6,8 +6,9 @@
 from jax.sharding import PartitionSpec as P
 
 ROUNDS = 4
-CHUNKS = 4
-ROUND_ORDER = (3, 0, 1, 2)
+CHUNKS = 2
+ROUND_ORDER = (3, 2, 1, 0)
+PEERS = (6, 7, 4, 5, 2, 3, 1)
 
 
 def split(value):
@@ -78,12 +79,18 @@
     block = lax.axis_index("res")
     seq = lax.axis_index("seq")
 
+    def flip(index, mask):
+        return index + mask - 2 * mask * ((index // mask) % 2)
+
     def partner(step):
-        mask = 1 << step
-        return block + mask - 2 * mask * ((block // mask) % 2)
+        return flip(block, 1 << step)
 
     def peer(offset):
-        return (seq + offset) % seq_devices
+        result = seq
+        for mask in (1, 2, 4):
+            if offset & mask:
+                result = flip(result, mask)
+        return result
 
     loads = []
     for index, (source, target) in enumerate(
@@ -147,7 +154,10 @@
             )
         if chunk == 0:
             pl.semaphore_wait(barrier, ROUNDS + seq_devices - 1)
-        for step in (2, 1, 0, 3):
+        for step in (2, 3):
+            right_copy(step, chunk).start()
+    for step in (1, 0):
+        for chunk in range(CHUNKS):
             right_copy(step, chunk).start()
 
     seq_group = group_index(local_seqs, hidden)
@@ -204,7 +214,7 @@
         product = matmul(jnp.concatenate([flat_high, flat_low], axis=0), weight_split[...])
         total = (product[64:, 128:] + product[64:, :128]) + (product[:64, 128:] + product[:64, :128])
         tiles[step] = total.reshape(8, 8, 128)
-        for offset in range(1, seq_devices):
+        for offset in PEERS:
             sum_copy(step, offset).start()
 
     for step in ROUND_ORDER:
@@ -229,7 +239,7 @@
     dma = pltpu.SemaphoreType.DMA
     out = pl.pallas_call(
         kernel,
-        out_shape=jax.ShapeDtypeStruct((ROUNDS, 8, 128), f32),
+        out_shape=pltpu.VMEM((ROUNDS, 8, 128), f32),
         in_specs=[pl.BlockSpec(memory_space=pltpu.HBM)] * 6,
         out_specs=pl.BlockSpec(memory_space=pltpu.VMEM),
         scratch_shapes=[
@@ -261,12 +271,17 @@
             collective_id=0, has_side_effects=True, vmem_limit_bytes=32 * 1024 * 1024
         ),
     )(
-        features.reshape(rows, channels),
-        gain.reshape(1, channels),
-        left_weight.T,
-        right_weight.T,
-        weight,
-        bias.reshape(1, 128),
+        *(
+            pltpu.with_memory_space_constraint(operand, pltpu.HBM)
+            for operand in (
+                features.reshape(rows, channels),
+                gain.reshape(1, channels),
+                left_weight.T,
+                right_weight.T,
+                weight,
+                bias.reshape(1, 128),
+            )
+        )
     )
     return out.reshape(ROUNDS, 8, 1, 128)
 

time: 30.9 us -> 25 us (0.81)
  local copies, waits for them, and re-layouts: 4.89 us -> 0.61 us
  Pallas kernels: 25.6 us -> 24.3 us
    unnamed x13 -> x1, local copies, waits for them, and re-layouts: 4.89 us -> 0.61 us
    pallas_call x1, Pallas kernels: 25.6 us -> 24.3 us  [on_device(): pl.pallas_call(kernel, out_shape=pltpu.VMEM((ROUNDS, 8, 128), f32), in_sp...]
where the time goes in v2:
time: 25 us; the launch traced here: 24.9 us
  Pallas kernels  24.3 us (97%)
  local copies, waits for them, and re-layouts  0.61 us (2%)
    pallas_call x1, Pallas kernels, on_device(): pl.pallas_call(kernel, out_shape=pltpu.VMEM((ROUNDS, 8, 128), f32), in_sp...  24.3 us
    unnamed x1, local copies, waits for them, and re-layouts  0.61 us

profile of v2, /device:TPU:1, one launch (start us, length us, event | category | flops | bytes accessed | tf_op | source)
XLA Modules:
  0.0 24.9 jit_solution(1603583685319999665)
XLA Ops:
  0.0 24.3 %shard_map.64 = f32[4,8,128]{2,1,0:T(8,128)S(1)} custom-call(f32[512,256]{1,0:T(8,128)} %bitcast.9, f32[1,256]{1,0:T(1,128)} %bitcast.12, f32[32,256]{1,0:T(8,128)} %bitcast.10, f32[32,256]{1,0:T(8,128)} %bitcast.11, f32[1024,128]{1,0:T(8,128)} %weight_hbm.1, f32[1,128]{1,0:T(1,128)} %bitcast.13), custom_call_target="tpu_custom_call" | custom-call | tf_op jit(solution)/shard_map/pallas_call | solution.py:240
  24.3 0.6 %copy.9 = f32[4,8,1,128]{3,2,1,0:T(1,128)} copy(f32[4,8,1,128]{3,2,1,0:T(1,128)S(1)} %bitcast.8) | data formatting | bytes 32768

commit v3 on v2

--- a/solution.py
+++ b/solution.py
@@ -6,7 +6,7 @@
 from jax.sharding import PartitionSpec as P
 
 ROUNDS = 4
-CHUNKS = 2
+SEND_ORDER = (3, 2, 1, 0)
 ROUND_ORDER = (3, 2, 1, 0)
 PEERS = (6, 7, 4, 5, 2, 3, 1)
 
@@ -69,8 +69,6 @@
     sum_recv_sem,
 ):
     rows = features.shape[0]
-    chunk_rows = rows // CHUNKS
-    chunk_seqs = chunk_rows // 8
     local_seqs = rows // 8
     hidden = 32
     seq_devices = 8
@@ -92,20 +90,20 @@
                 result = flip(result, mask)
         return result
 
-    loads = []
-    for index, (source, target) in enumerate(
-        ((left_hbm, left_weight), (right_hbm, right_weight), (gain_hbm, gain))
-    ):
-        loads.append(pltpu.make_async_copy(source, target, in_sem.at[index]))
-    chunk_loads = []
-    for chunk in range(CHUNKS):
-        part = pl.ds(chunk * chunk_rows, chunk_rows)
-        chunk_loads.append(
-            pltpu.make_async_copy(features_hbm.at[part], features.at[part], in_sem.at[5 + chunk])
-        )
-    weight_load = pltpu.make_async_copy(weight_hbm, weight, in_sem.at[3])
-    bias_load = pltpu.make_async_copy(bias_hbm, bias, in_sem.at[4])
-    for copy in loads + chunk_loads + [weight_load, bias_load]:
+    copies = [
+        pltpu.make_async_copy(source, target, in_sem.at[index])
+        for index, (source, target) in enumerate(
+            (
+                (features_hbm, features),
+                (left_hbm, left_weight),
+                (right_hbm, right_weight),
+                (gain_hbm, gain),
+                (weight_hbm, weight),
+                (bias_hbm, bias),
+            )
+        )
+    ]
+    for copy in copies:
         copy.start()
 
     barrier = pltpu.get_barrier_semaphore()
@@ -114,53 +112,40 @@
     for offset in range(1, seq_devices):
         pl.semaphore_signal(barrier, inc=1, device_id=(block, peer(offset)))
 
-    for copy in loads:
+    for copy in copies[1:4]:
         copy.wait()
     left_high, left_low = split(left_weight[...] * gain[...])
     right_high, right_low = split(right_weight[...] * gain[...])
     proj_high[...] = jnp.concatenate([left_high] * 4 + [right_high] * 4, axis=0)
     proj_low[...] = jnp.concatenate([left_low] * 4 + [right_low] * 4, axis=0)
 
-    def right_copy(step, chunk):
-        part = pl.ds(chunk * chunk_seqs, chunk_seqs)
+    def right_copy(step):
         return pltpu.make_async_remote_copy(
-            src_ref=right_mine.at[part],
-            dst_ref=right_got.at[step, part],
-            send_sem=right_send_sem.at[step, chunk],
-            recv_sem=right_recv_sem.at[step, chunk],
+            src_ref=right_mine,
+            dst_ref=right_got.at[step],
+            send_sem=right_send_sem,
+            recv_sem=right_recv_sem.at[step],
             device_id=(partner(step), seq),
         )
 
-    chunk_group = group_index(chunk_seqs, hidden)
-    for chunk in range(CHUNKS):
-        chunk_loads[chunk].wait()
-        part = pl.ds(chunk * chunk_rows, chunk_rows)
-        values = features[part]
-        centered = values - jnp.mean(values, axis=1, keepdims=True)
-        variance = jnp.mean(centered * centered, axis=1, keepdims=True)
-        high, low = split(centered * lax.rsqrt(variance + 1e-05))
-        projected = (
-            matmul_nt(high, proj_low[...]) + matmul_nt(low, proj_high[...])
-        ) + matmul_nt(high, proj_high[...])
-        left_rows[part] = projected[:, :128]
-        right_rows[part] = projected[:, 128:]
-        for half in range(2):
-            lanes = [
-                right_rows[pl.ds(chunk * chunk_rows + half * 4 + x, chunk_seqs, stride=8), :]
-                for x in range(4)
-            ]
-            right_mine[pl.ds(chunk * chunk_seqs, chunk_seqs), pl.ds(half * 128, 128)] = pick(
-                lanes, chunk_group
-            )
-        if chunk == 0:
-            pl.semaphore_wait(barrier, ROUNDS + seq_devices - 1)
-        for step in (2, 3):
-            right_copy(step, chunk).start()
-    for step in (1, 0):
-        for chunk in range(CHUNKS):
-            right_copy(step, chunk).start()
-
+    copies[0].wait()
+    values = features[...]
+    centered = values - jnp.mean(values, axis=1, keepdims=True)
+    variance = jnp.mean(centered * centered, axis=1, keepdims=True)
+    high, low = split(centered * lax.rsqrt(variance + 1e-05))
+    projected = (
+        matmul_nt(high, proj_low[...]) + matmul_nt(low, proj_high[...])
+    ) + matmul_nt(high, proj_high[...])
+    left_rows[...] = projected[:, :128]
+    right_rows[...] = projected[:, 128:]
     seq_group = group_index(local_seqs, hidden)
+    for half in range(2):
+        lanes = [right_rows[pl.ds(half * 4 + x, local_seqs, stride=8), :] for x in range(4)]
+        right_mine[:, pl.ds(half * 128, 128)] = pick(lanes, seq_group)
+    pl.semaphore_wait(barrier, ROUNDS + seq_devices - 1)
+    for step in SEND_ORDER:
+        right_copy(step).start()
+
     for half in range(2):
         lanes = [left_rows[pl.ds(half * 4 + x, local_seqs, stride=8), :] for x in range(4)]
         left_half = pick(lanes, seq_group) * (1.0 / total_seqs)
@@ -171,8 +156,8 @@
     turned_high, turned_low = split(left_columns)
     left_parts[...] = jnp.concatenate([turned_high, turned_low], axis=1)
 
-    weight_load.wait()
-    bias_load.wait()
+    for copy in copies[4:]:
+        copy.wait()
     weight_high, weight_low = split(weight[...])
     weight_split[...] = jnp.concatenate([weight_high, weight_low], axis=1)
 
@@ -180,15 +165,14 @@
         return pltpu.make_async_remote_copy(
             src_ref=tiles.at[step, peer(offset)],
             dst_ref=sums.at[step, offset - 1],
-            send_sem=sum_send_sem.at[step, offset - 1],
-            recv_sem=sum_recv_sem.at[step, offset - 1],
+            send_sem=sum_send_sem,
+            recv_sem=sum_recv_sem,
             device_id=(block, peer(offset)),
         )
 
     group = group_index(8, hidden)
     for step in ROUND_ORDER:
-        for chunk in range(CHUNKS):
-            right_copy(step, chunk).wait_recv()
+        right_copy(step).wait_recv()
         right_high, right_low = split(right_got[step])
         outer[...] = matmul(
             left_parts[...],
@@ -217,19 +201,14 @@
         for offset in PEERS:
             sum_copy(step, offset).start()
 
-    for step in ROUND_ORDER:
-        for offset in range(1, seq_devices):
-            sum_copy(step, offset).wait_recv()
+    pltpu.make_async_copy(right_got, right_got, right_send_sem).wait()
+    pltpu.make_async_copy(sums, sums, sum_send_sem).wait()
+    pltpu.make_async_copy(sums, sums, sum_recv_sem).wait()
+    for step in range(ROUNDS):
         total = tiles[step, seq] + bias[...]
         for offset in range(1, seq_devices):
             total = total + sums[step, offset - 1]
         out_ref[step] = total
-
-    for step in range(ROUNDS):
-        for chunk in range(CHUNKS):
-            right_copy(step, chunk).wait_send()
-        for offset in range(1, seq_devices):
-            sum_copy(step, offset).wait_send()
 
 
 def on_device(features, gain, left_weight, right_weight, weight, bias):
@@ -249,7 +228,7 @@
             pltpu.VMEM((32, channels), f32),
             pltpu.VMEM((1024, 128), f32),
             pltpu.VMEM((1, 128), f32),
-            dma((5 + CHUNKS,)),
+            dma((6,)),
             pltpu.VMEM((256, channels), bf16),
             pltpu.VMEM((256, channels), bf16),
             pltpu.VMEM((1024, 256), bf16),
@@ -262,10 +241,10 @@
             pltpu.VMEM((256, 256), f32),
             pltpu.VMEM((ROUNDS, 8, 8, 128), f32),
             pltpu.VMEM((ROUNDS, 7, 8, 128), f32),
-            dma((ROUNDS, CHUNKS)),
-            dma((ROUNDS, CHUNKS)),
-            dma((ROUNDS, 7)),
-            dma((ROUNDS, 7)),
+            dma,
+            dma((ROUNDS,)),
+            dma,
+            dma,
         ],
         compiler_params=pltpu.CompilerParams(
             collective_id=0, has_side_effects=True, vmem_limit_bytes=32 * 1024 * 1024

time: 25 us -> 24 us (0.960)
  Pallas kernels: 24.3 us -> 23.3 us
    pallas_call x1, Pallas kernels: 24.3 us -> 23.3 us  [on_device(): pl.pallas_call(kernel, out_shape=pltpu.VMEM((ROUNDS, 8, 128), f32), in_sp...]
where the time goes in v3:
time: 24 us; the launch traced here: 23.9 us
  Pallas kernels  23.3 us (97%)
  local copies, waits for them, and re-layouts  0.61 us (3%)
    pallas_call x1, Pallas kernels, on_device(): pl.pallas_call(kernel, out_shape=pltpu.VMEM((ROUNDS, 8, 128), f32), in_sp...  23.3 us
    unnamed x1, local copies, waits for them, and re-layouts  0.61 us

profile of v3, /device:TPU:1, one launch (start us, length us, event | category | flops | bytes accessed | tf_op | source)
XLA Modules:
  0.0 23.9 jit_solution(5028259732713293969)
XLA Ops:
  0.0 23.3 %shard_map.64 = f32[4,8,128]{2,1,0:T(8,128)S(1)} custom-call(f32[512,256]{1,0:T(8,128)} %bitcast.9, f32[1,256]{1,0:T(1,128)} %bitcast.12, f32[32,256]{1,0:T(8,128)} %bitcast.10, f32[32,256]{1,0:T(8,128)} %bitcast.11, f32[1024,128]{1,0:T(8,128)} %weight_hbm.1, f32[1,128]{1,0:T(1,128)} %bitcast.13), custom_call_target="tpu_custom_call" | custom-call | tf_op jit(solution)/shard_map/pallas_call | solution.py:219
  23.3 0.6 %copy.9 = f32[4,8,1,128]{3,2,1,0:T(1,128)} copy(f32[4,8,1,128]{3,2,1,0:T(1,128)S(1)} %bitcast.8) | data formatting | bytes 32768

commit v4 on v3

--- a/solution.py
+++ b/solution.py
@@ -8,6 +8,11 @@
 ROUNDS = 4
 SEND_ORDER = (3, 2, 1, 0)
 ROUND_ORDER = (3, 2, 1, 0)
+MASKS = (1, 2, 6, 8)
+HELD = (0, 1, 1, 3)
+FAR = 2
+SUMS = 29
+NEAR_SLOT = (0, 1, None, 2)
 PEERS = (6, 7, 4, 5, 2, 3, 1)
 
 
@@ -58,6 +63,7 @@
     right_rows,
     left_turned,
     left_parts,
+    left_mine,
     right_mine,
     right_got,
     outer,
@@ -78,17 +84,20 @@
     seq = lax.axis_index("seq")
 
     def flip(index, mask):
-        return index + mask - 2 * mask * ((index // mask) % 2)
+        result = index
+        for bit in (1, 2, 4, 8):
+            if mask & bit:
+                result = result + bit - 2 * bit * ((index // bit) % 2)
+        return result
 
     def partner(step):
-        return flip(block, 1 << step)
+        return flip(block, MASKS[step])
 
     def peer(offset):
-        result = seq
-        for mask in (1, 2, 4):
-            if offset & mask:
-                result = flip(result, mask)
-        return result
+        return flip(seq, offset)
+
+    def sum_peers(step):
+        return PEERS + (0,) if step == FAR else PEERS
 
     copies = [
         pltpu.make_async_copy(source, target, in_sem.at[index])
@@ -109,7 +118,8 @@
     barrier = pltpu.get_barrier_semaphore()
     for step in range(ROUNDS):
         pl.semaphore_signal(barrier, inc=1, device_id=(partner(step), seq))
-    for offset in range(1, seq_devices):
+    for offset in PEERS:
+        pl.semaphore_signal(barrier, inc=1, device_id=(partner(FAR), peer(offset)))
         pl.semaphore_signal(barrier, inc=1, device_id=(block, peer(offset)))
 
     for copy in copies[1:4]:
@@ -121,7 +131,7 @@
 
     def right_copy(step):
         return pltpu.make_async_remote_copy(
-            src_ref=right_mine,
+            src_ref=left_mine if step == FAR else right_mine,
             dst_ref=right_got.at[step],
             send_sem=right_send_sem,
             recv_sem=right_recv_sem.at[step],
@@ -139,43 +149,62 @@
     left_rows[...] = projected[:, :128]
     right_rows[...] = projected[:, 128:]
     seq_group = group_index(local_seqs, hidden)
-    for half in range(2):
-        lanes = [right_rows[pl.ds(half * 4 + x, local_seqs, stride=8), :] for x in range(4)]
-        right_mine[:, pl.ds(half * 128, 128)] = pick(lanes, seq_group)
-    pl.semaphore_wait(barrier, ROUNDS + seq_devices - 1)
+    for source, target, scale in (
+        (left_rows, left_mine, 1.0 / total_seqs),
+        (right_rows, right_mine, 1.0),
+    ):
+        for half in range(2):
+            lanes = [source[pl.ds(half * 4 + x, local_seqs, stride=8), :] for x in range(4)]
+            target[:, pl.ds(half * 128, 128)] = pick(lanes, seq_group) * scale
+    pl.semaphore_wait(barrier, ROUNDS + 2 * (seq_devices - 1))
     for step in SEND_ORDER:
         right_copy(step).start()
 
-    for half in range(2):
-        lanes = [left_rows[pl.ds(half * 4 + x, local_seqs, stride=8), :] for x in range(4)]
-        left_half = pick(lanes, seq_group) * (1.0 / total_seqs)
-        left_turned[pl.ds(half * 128, 128), :] = jnp.concatenate([left_half, left_half], axis=0).T
-    left_columns = jnp.concatenate(
-        [left_turned[pl.ds(c, 8, stride=hidden), :] for c in range(hidden)], axis=0
-    )
-    turned_high, turned_low = split(left_columns)
-    left_parts[...] = jnp.concatenate([turned_high, turned_low], axis=1)
+    def turn_left(rows):
+        for half in range(2):
+            left_half = rows[:, half * 128 : half * 128 + 128]
+            left_turned[pl.ds(half * 128, 128), :] = jnp.concatenate(
+                [left_half, left_half], axis=0
+            ).T
+        left_columns = jnp.concatenate(
+            [left_turned[pl.ds(c, 8, stride=hidden), :] for c in range(hidden)], axis=0
+        )
+        turned_high, turned_low = split(left_columns)
+        return jnp.concatenate([turned_high, turned_low], axis=1)
+
+    left_parts[...] = turn_left(left_mine[...])
 
     for copy in copies[4:]:
         copy.wait()
     weight_high, weight_low = split(weight[...])
     weight_split[...] = jnp.concatenate([weight_high, weight_low], axis=1)
 
+    def sum_slot(step, offset):
+        if step == FAR:
+            return SUMS - seq_devices + offset
+        return NEAR_SLOT[step] * (seq_devices - 1) + offset - 1
+
     def sum_copy(step, offset):
         return pltpu.make_async_remote_copy(
             src_ref=tiles.at[step, peer(offset)],
-            dst_ref=sums.at[step, offset - 1],
+            dst_ref=sums.at[sum_slot(step, offset)],
             send_sem=sum_send_sem,
             recv_sem=sum_recv_sem,
-            device_id=(block, peer(offset)),
+            device_id=(partner(FAR) if step == FAR else block, peer(offset)),
         )
 
     group = group_index(8, hidden)
     for step in ROUND_ORDER:
-        right_copy(step).wait_recv()
-        right_high, right_low = split(right_got[step])
+        if step != HELD[FAR]:
+            right_copy(step).wait_recv()
+        if step == FAR:
+            left = turn_left(right_got[FAR])
+            right_copy(HELD[FAR]).wait_recv()
+        else:
+            left = left_parts[...]
+        right_high, right_low = split(right_got[HELD[step]])
         outer[...] = matmul(
-            left_parts[...],
+            left,
             jnp.concatenate([right_high, right_low, right_high, right_low], axis=0),
         )
         pieces = []
@@ -198,16 +227,16 @@
         product = matmul(jnp.concatenate([flat_high, flat_low], axis=0), weight_split[...])
         total = (product[64:, 128:] + product[64:, :128]) + (product[:64, 128:] + product[:64, :128])
         tiles[step] = total.reshape(8, 8, 128)
-        for offset in PEERS:
+        for offset in sum_peers(step):
             sum_copy(step, offset).start()
 
     pltpu.make_async_copy(right_got, right_got, right_send_sem).wait()
     pltpu.make_async_copy(sums, sums, sum_send_sem).wait()
     pltpu.make_async_copy(sums, sums, sum_recv_sem).wait()
     for step in range(ROUNDS):
-        total = tiles[step, seq] + bias[...]
-        for offset in range(1, seq_devices):
-            total = total + sums[step, offset - 1]
+        total = bias[...] if step == FAR else tiles[step, seq] + bias[...]
+        for offset in sum_peers(step):
+            total = total + sums[sum_slot(step, offset)]
         out_ref[step] = total
 
 
@@ -237,10 +266,11 @@
             pltpu.VMEM((256, 128), f32),
             pltpu.VMEM((256, 256), bf16),
             pltpu.VMEM((local_seqs, 256), f32),
+            pltpu.VMEM((local_seqs, 256), f32),
             pltpu.VMEM((ROUNDS, local_seqs, 256), f32),
             pltpu.VMEM((256, 256), f32),
             pltpu.VMEM((ROUNDS, 8, 8, 128), f32),
-            pltpu.VMEM((ROUNDS, 7, 8, 128), f32),
+            pltpu.VMEM((SUMS, 8, 128), f32),
             dma,
             dma((ROUNDS,)),
             dma,

time: 24 us -> 23.1 us (0.963)
  Pallas kernels: 23.3 us -> 22.3 us
    pallas_call x1, Pallas kernels: 23.3 us -> 22.3 us  [on_device(): pl.pallas_call(kernel, out_shape=pltpu.VMEM((ROUNDS, 8, 128), f32), in_sp...]
where the time goes in v4:
time: 23.1 us; the launch traced here: 22.9 us
  Pallas kernels  22.3 us (97%)
  local copies, waits for them, and re-layouts  0.61 us (3%)
    pallas_call x1, Pallas kernels, on_device(): pl.pallas_call(kernel, out_shape=pltpu.VMEM((ROUNDS, 8, 128), f32), in_sp...  22.3 us
    unnamed x1, local copies, waits for them, and re-layouts  0.61 us

profile of v4, /device:TPU:1, one launch (start us, length us, event | category | flops | bytes accessed | tf_op | source)
XLA Modules:
  0.0 22.9 jit_solution(9866245392659427217)
XLA Ops:
  0.0 22.3 %shard_map.64 = f32[4,8,128]{2,1,0:T(8,128)S(1)} custom-call(f32[512,256]{1,0:T(8,128)} %bitcast.9, f32[1,256]{1,0:T(1,128)} %bitcast.12, f32[32,256]{1,0:T(8,128)} %bitcast.10, f32[32,256]{1,0:T(8,128)} %bitcast.11, f32[1024,128]{1,0:T(8,128)} %weight_hbm.1, f32[1,128]{1,0:T(1,128)} %bitcast.13), custom_call_target="tpu_custom_call" | custom-call | tf_op jit(solution)/shard_map/pallas_call | solution.py:248
  22.3 0.6 %copy.9 = f32[4,8,1,128]{3,2,1,0:T(1,128)} copy(f32[4,8,1,128]{3,2,1,0:T(1,128)S(1)} %bitcast.8) | data formatting | bytes 32768

commit v5 on v4

--- a/solution.py
+++ b/solution.py
@@ -14,6 +14,7 @@
 SUMS = 29
 NEAR_SLOT = (0, 1, None, 2)
 PEERS = (6, 7, 4, 5, 2, 3, 1)
+GREETED = (4, 5, 2, 3, 1)
 
 
 def split(value):
@@ -73,6 +74,8 @@
     right_recv_sem,
     sum_send_sem,
     sum_recv_sem,
+    peers_ready,
+    far_ready,
 ):
     rows = features.shape[0]
     local_seqs = rows // 8
@@ -118,8 +121,7 @@
     barrier = pltpu.get_barrier_semaphore()
     for step in range(ROUNDS):
         pl.semaphore_signal(barrier, inc=1, device_id=(partner(step), seq))
-    for offset in PEERS:
-        pl.semaphore_signal(barrier, inc=1, device_id=(partner(FAR), peer(offset)))
+    for offset in GREETED:
         pl.semaphore_signal(barrier, inc=1, device_id=(block, peer(offset)))
 
     for copy in copies[1:4]:
@@ -156,9 +158,11 @@
         for half in range(2):
             lanes = [source[pl.ds(half * 4 + x, local_seqs, stride=8), :] for x in range(4)]
             target[:, pl.ds(half * 128, 128)] = pick(lanes, seq_group) * scale
-    pl.semaphore_wait(barrier, ROUNDS + 2 * (seq_devices - 1))
+    pl.semaphore_wait(barrier, ROUNDS + len(GREETED))
     for step in SEND_ORDER:
         right_copy(step).start()
+    for offset in GREETED:
+        pl.semaphore_signal(peers_ready, inc=1, device_id=(block, peer(offset)))
 
     def turn_left(rows):
         for half in range(2):
@@ -178,6 +182,9 @@
         copy.wait()
     weight_high, weight_low = split(weight[...])
     weight_split[...] = jnp.concatenate([weight_high, weight_low], axis=1)
+
+    pl.semaphore_wait(peers_ready, len(GREETED))
+    pl.semaphore_signal(far_ready, inc=1, device_id=(partner(FAR), seq))
 
     def sum_slot(step, offset):
         if step == FAR:
@@ -227,6 +234,8 @@
         product = matmul(jnp.concatenate([flat_high, flat_low], axis=0), weight_split[...])
         total = (product[64:, 128:] + product[64:, :128]) + (product[:64, 128:] + product[:64, :128])
         tiles[step] = total.reshape(8, 8, 128)
+        if step == FAR:
+            pl.semaphore_wait(far_ready, 1)
         for offset in sum_peers(step):
             sum_copy(step, offset).start()
 
@@ -275,6 +284,8 @@
             dma((ROUNDS,)),
             dma,
             dma,
+            pltpu.SemaphoreType.REGULAR,
+            pltpu.SemaphoreType.REGULAR,
         ],
         compiler_params=pltpu.CompilerParams(
             collective_id=0, has_side_effects=True, vmem_limit_bytes=32 * 1024 * 1024

time: 23.1 us -> 22.7 us (0.983)
  Pallas kernels: 22.3 us -> 22 us
    pallas_call x1, Pallas kernels: 22.3 us -> 22 us  [on_device(): pl.pallas_call(kernel, out_shape=pltpu.VMEM((ROUNDS, 8, 128), f32), in_sp...]
where the time goes in v5:
time: 22.7 us; the launch traced here: 22.6 us
  Pallas kernels  22 us (97%)
  local copies, waits for them, and re-layouts  0.61 us (3%)
    pallas_call x1, Pallas kernels, on_device(): pl.pallas_call(kernel, out_shape=pltpu.VMEM((ROUNDS, 8, 128), f32), in_sp...  22 us
    unnamed x1, local copies, waits for them, and re-layouts  0.61 us

profile of v5, /device:TPU:1, one launch (start us, length us, event | category | flops | bytes accessed | tf_op | source)
XLA Modules:
  0.0 22.6 jit_solution(18443475398041003009)
XLA Ops:
  0.0 22.0 %shard_map.64 = f32[4,8,128]{2,1,0:T(8,128)S(1)} custom-call(f32[512,256]{1,0:T(8,128)} %bitcast.9, f32[1,256]{1,0:T(1,128)} %bitcast.12, f32[32,256]{1,0:T(8,128)} %bitcast.10, f32[32,256]{1,0:T(8,128)} %bitcast.11, f32[1024,128]{1,0:T(8,128)} %weight_hbm.1, f32[1,128]{1,0:T(1,128)} %bitcast.13), custom_call_target="tpu_custom_call" | custom-call | tf_op jit(solution)/shard_map/pallas_call | solution.py:257
  22.0 0.6 %copy.9 = f32[4,8,1,128]{3,2,1,0:T(1,128)} copy(f32[4,8,1,128]{3,2,1,0:T(1,128)S(1)} %bitcast.8) | data formatting | bytes 32768

commit v6 on v5

--- a/solution.py
+++ b/solution.py
@@ -6,8 +6,10 @@
 from jax.sharding import PartitionSpec as P
 
 ROUNDS = 4
-SEND_ORDER = (3, 2, 1, 0)
-ROUND_ORDER = (3, 2, 1, 0)
+EARLY_SENDS = (3, 2, 1, 0)
+LATE_SENDS = (3, 1, 2, 0)
+EARLY_ROUNDS = (1, 0, 2)
+LATE_ROUNDS = (2, 1, 0)
 MASKS = (1, 2, 6, 8)
 HELD = (0, 1, 1, 3)
 FAR = 2
@@ -159,8 +161,18 @@
             lanes = [source[pl.ds(half * 4 + x, local_seqs, stride=8), :] for x in range(4)]
             target[:, pl.ds(half * 128, 128)] = pick(lanes, seq_group) * scale
     pl.semaphore_wait(barrier, ROUNDS + len(GREETED))
-    for step in SEND_ORDER:
-        right_copy(step).start()
+    early = block % 8 < 4
+
+    @pl.when(early)
+    def _():
+        for step in EARLY_SENDS:
+            right_copy(step).start()
+
+    @pl.when(jnp.logical_not(early))
+    def _():
+        for step in LATE_SENDS:
+            right_copy(step).start()
+
     for offset in GREETED:
         pl.semaphore_signal(peers_ready, inc=1, device_id=(block, peer(offset)))
 
@@ -201,12 +213,13 @@
         )
 
     group = group_index(8, hidden)
-    for step in ROUND_ORDER:
-        if step != HELD[FAR]:
+    def compute_round(step, arrived):
+        if step not in arrived:
             right_copy(step).wait_recv()
         if step == FAR:
             left = turn_left(right_got[FAR])
-            right_copy(HELD[FAR]).wait_recv()
+            if HELD[FAR] not in arrived:
+                right_copy(HELD[FAR]).wait_recv()
         else:
             left = left_parts[...]
         right_high, right_low = split(right_got[HELD[step]])
@@ -238,6 +251,18 @@
             pl.semaphore_wait(far_ready, 1)
         for offset in sum_peers(step):
             sum_copy(step, offset).start()
+
+    compute_round(3, ())
+
+    @pl.when(early)
+    def _():
+        for index, step in enumerate(EARLY_ROUNDS):
+            compute_round(step, EARLY_ROUNDS[:index])
+
+    @pl.when(jnp.logical_not(early))
+    def _():
+        for index, step in enumerate(LATE_ROUNDS):
+            compute_round(step, (HELD[FAR],) if index else ())
 
     pltpu.make_async_copy(right_got, right_got, right_send_sem).wait()
     pltpu.make_async_copy(sums, sums, sum_send_sem).wait()

time: 22.7 us -> 22.7 us (level)
  no operation moved by 1% of the time
where the time goes in v6:
time: 22.7 us; the launch traced here: 22.5 us
  Pallas kernels  21.9 us (96%)
  local copies, waits for them, and re-layouts  0.61 us (3%)
    pallas_call x1, Pallas kernels, on_device(): pl.pallas_call(kernel, out_shape=pltpu.VMEM((ROUNDS, 8, 128), f32), in_sp...  21.9 us
    unnamed x1, local copies, waits for them, and re-layouts  0.61 us

profile of v6, /device:TPU:1, one launch (start us, length us, event | category | flops | bytes accessed | tf_op | source)
XLA Modules:
  0.0 22.5 jit_solution(16165103280970403270)
XLA Ops:
  0.0 21.9 %shard_map.64 = f32[4,8,128]{2,1,0:T(8,128)S(1)} custom-call(f32[512,256]{1,0:T(8,128)} %bitcast.9, f32[1,256]{1,0:T(1,128)} %bitcast.12, f32[32,256]{1,0:T(8,128)} %bitcast.10, f32[32,256]{1,0:T(8,128)} %bitcast.11, f32[1024,128]{1,0:T(8,128)} %weight_hbm.1, f32[1,128]{1,0:T(1,128)} %bitcast.13), custom_call_target="tpu_custom_call" | custom-call | tf_op jit(solution)/shard_map/pallas_call | solution.py:282
  21.9 0.6 %copy.9 = f32[4,8,1,128]{3,2,1,0:T(1,128)} copy(f32[4,8,1,128]{3,2,1,0:T(1,128)S(1)} %bitcast.8) | data formatting | bytes 32768

commit v7 on v6

--- a/solution.py
+++ b/solution.py
@@ -8,8 +8,8 @@
 ROUNDS = 4
 EARLY_SENDS = (3, 2, 1, 0)
 LATE_SENDS = (3, 1, 2, 0)
-EARLY_ROUNDS = (1, 0, 2)
-LATE_ROUNDS = (2, 1, 0)
+EARLY_ROUNDS = (0, 1, 3, 2)
+LATE_ROUNDS = (2, 3, 1, 0)
 MASKS = (1, 2, 6, 8)
 HELD = (0, 1, 1, 3)
 FAR = 2
@@ -251,8 +251,6 @@
             pl.semaphore_wait(far_ready, 1)
         for offset in sum_peers(step):
             sum_copy(step, offset).start()
-
-    compute_round(3, ())
 
     @pl.when(early)
     def _():

time: 22.7 us -> 22.6 us (level)
  no operation moved by 1% of the time
where the time goes in v7:
time: 22.6 us; the launch traced here: 22.5 us
  Pallas kernels  21.8 us (96%)
  local copies, waits for them, and re-layouts  0.61 us (3%)
    pallas_call x1, Pallas kernels, on_device(): pl.pallas_call(kernel, out_shape=pltpu.VMEM((ROUNDS, 8, 128), f32), in_sp...  21.8 us
    unnamed x1, local copies, waits for them, and re-layouts  0.61 us

profile of v7, /device:TPU:1, one launch (start us, length us, event | category | flops | bytes accessed | tf_op | source)
XLA Modules:
  0.0 22.5 jit_solution(13402615695652303820)
XLA Ops:
  0.0 21.8 %shard_map.64 = f32[4,8,128]{2,1,0:T(8,128)S(1)} custom-call(f32[512,256]{1,0:T(8,128)} %bitcast.9, f32[1,256]{1,0:T(1,128)} %bitcast.12, f32[32,256]{1,0:T(8,128)} %bitcast.10, f32[32,256]{1,0:T(8,128)} %bitcast.11, f32[1024,128]{1,0:T(8,128)} %weight_hbm.1, f32[1,128]{1,0:T(1,128)} %bitcast.13), custom_call_target="tpu_custom_call" | custom-call | tf_op jit(solution)/shard_map/pallas_call | solution.py:280
  21.9 0.6 %copy.9 = f32[4,8,1,128]{3,2,1,0:T(1,128)} copy(f32[4,8,1,128]{3,2,1,0:T(1,128)S(1)} %bitcast.8) | data formatting | bytes 32768

commit v8 on v7

--- a/solution.py
+++ b/solution.py
@@ -8,7 +8,7 @@
 ROUNDS = 4
 EARLY_SENDS = (3, 2, 1, 0)
 LATE_SENDS = (3, 1, 2, 0)
-EARLY_ROUNDS = (0, 1, 3, 2)
+EARLY_ROUNDS = (0, 3, 1, 2)
 LATE_ROUNDS = (2, 3, 1, 0)
 MASKS = (1, 2, 6, 8)
 HELD = (0, 1, 1, 3)

time: 22.6 us -> 22.6 us (level)
  no operation moved by 1% of the time
where the time goes in v8:
time: 22.6 us; the launch traced here: 22.5 us
  Pallas kernels  21.8 us (96%)
  local copies, waits for them, and re-layouts  0.61 us (3%)
    pallas_call x1, Pallas kernels, on_device(): pl.pallas_call(kernel, out_shape=pltpu.VMEM((ROUNDS, 8, 128), f32), in_sp...  21.8 us
    unnamed x1, local copies, waits for them, and re-layouts  0.61 us

profile of v8, /device:TPU:1, one launch (start us, length us, event | category | flops | bytes accessed | tf_op | source)
XLA Modules:
  0.0 22.5 jit_solution(8761721894865912479)
XLA Ops:
  0.0 21.8 %shard_map.64 = f32[4,8,128]{2,1,0:T(8,128)S(1)} custom-call(f32[512,256]{1,0:T(8,128)} %bitcast.9, f32[1,256]{1,0:T(1,128)} %bitcast.12, f32[32,256]{1,0:T(8,128)} %bitcast.10, f32[32,256]{1,0:T(8,128)} %bitcast.11, f32[1024,128]{1,0:T(8,128)} %weight_hbm.1, f32[1,128]{1,0:T(1,128)} %bitcast.13), custom_call_target="tpu_custom_call" | custom-call | tf_op jit(solution)/shard_map/pallas_call | solution.py:280
  21.9 0.6 %copy.9 = f32[4,8,1,128]{3,2,1,0:T(1,128)} copy(f32[4,8,1,128]{3,2,1,0:T(1,128)S(1)} %bitcast.8) | data formatting | bytes 32768
